TPU v7x, 512 devices: a whole 4x4x16 slice. The times are simulated.
512 devices in a mesh: dp: 128 (over x, z, core), tensor: 4 (over y).
Axes of the slice: x: 4, y: 4, z: 16, core: 2. Of those that a mesh axis runs over, the one named last changes fastest.
Arguments:
- tokens: bfloat16 [32768, 2048], P('dp', 'tensor'), may hold values from -6 to 6
- expert_ids: int32 [32768, 2], P('dp'), may hold values from 0 to 127, as said below
- route_weights: float32 [32768, 2], P('dp'), may hold values from 0.2 to 1
- gate_weight: bfloat16 [128, 2048, 1024], P('dp', None, 'tensor'), may hold values from -0.125 to 0.125
- up_weight: bfloat16 [128, 2048, 1024], P('dp', None, 'tensor'), may hold values from -0.125 to 0.125
- down_weight: bfloat16 [128, 1024, 2048], P('dp', 'tensor'), may hold values from -0.1875 to 0.1875
Outputs:
- moe_out: bfloat16 [32768, 2048], P('dp', 'tensor')
Inputs may be any that keep to these rules, and one draw needn't show every extreme that they name: `expert_ids`: the two experts of a row differ. Among the rows of one index of dp, no expert is named more than 8 times.
All inputs are finite; a program needn't handle non-finite values.
Results may differ from a plain program's by a relative error of at most 0.011.
Values may be sent and summed in bfloat16 or wider, within the bound.
A program may use at most 64 MiB of HBM per device.

v0:
```python
import jax
import jax.numpy as jnp
from jax import lax
from jax.sharding import PartitionSpec as P


def body(tokens, expert_ids, route_weights, gate_weight, up_weight, down_weight):
    tok_count = tokens.shape[0]
    local_experts = gate_weight.shape[0]
    model_width = gate_weight.shape[1]
    groups = lax.axis_size("dp")
    experts_all = local_experts * groups
    capacity = 4 * tok_count // groups
    chosen = expert_ids.reshape(-1)
    onehot = (chosen[:, None] == jnp.arange(experts_all, dtype=jnp.int32)[None, :]).astype(
        jnp.int32
    )
    earlier = jnp.cumsum(onehot, axis=0) - onehot
    slot_index = jnp.sum(earlier * onehot, axis=1)
    flat_slot = chosen * capacity + slot_index
    source_rows = tokens[jnp.arange(chosen.shape[0], dtype=jnp.int32) // 2]
    send_buffer = (
        jnp.zeros((experts_all * capacity, tokens.shape[1]), jnp.bfloat16)
        .at[flat_slot]
        .set(source_rows)
    )
    send_buffer = send_buffer.reshape(experts_all, 1, capacity, tokens.shape[1])
    features = lax.all_gather(
        lax.all_to_all(send_buffer, "dp", split_axis=0, concat_axis=1, tiled=True),
        "tensor",
        axis=3,
        tiled=True,
    )
    slot_count = features.shape[2]
    token_rows = features[0].reshape(-1, model_width)
    gate_value = jnp.dot(token_rows, gate_weight[0], preferred_element_type=jnp.float32)
    up_value = jnp.dot(token_rows, up_weight[0], preferred_element_type=jnp.float32)
    hidden = (jax.nn.silu(gate_value) * up_value).astype(jnp.bfloat16)
    partial_sum = jnp.dot(hidden, down_weight[0], preferred_element_type=jnp.float32)
    results = [partial_sum.reshape(features.shape[1], slot_count, model_width)]
    partial_out = jnp.stack(results, axis=0)
    reduced = lax.psum_scatter(
        partial_out.astype(jnp.bfloat16), "tensor", scatter_dimension=3, tiled=True
    )
    came_back = lax.all_to_all(reduced, "dp", split_axis=1, concat_axis=0, tiled=True)
    quarter_width = came_back.shape[3]
    result_table = came_back.reshape(experts_all * capacity, quarter_width)
    picked = result_table[flat_slot].astype(jnp.float32).reshape(tok_count, 2, quarter_width)
    mixed_out = jnp.sum(picked * route_weights[:, :, None], axis=1)
    return mixed_out.astype(jnp.bfloat16)


def solution(mesh):
    return jax.shard_map(
        body,
        mesh=mesh,
        in_specs=(
            P("dp", "tensor"),
            P("dp", None),
            P("dp", None),
            P("dp", None, "tensor"),
            P("dp", None, "tensor"),
            P("dp", "tensor", None),
        ),
        out_specs=P("dp", "tensor"),
        check_vma=False,
    )
```

profile of v0, /device:TPU:2, one launch (start us, length us, event | category | flops | bytes accessed | tf_op | source)
XLA Modules:
  0.0 289.4 jit_solution(14001448226767223536)
XLA Ops:
  6.5 0.0 copy-start
  6.5 0.0 all-gather.3.cloned.1.call-start
  6.5 1.0 copy.18
  7.5 0.1 eq.29
  7.7 0.1 eq.25
  7.8 0.7 broadcast_multiply_fusion
  8.5 0.1 copy.20
  8.6 0.2 fusion.22
  8.9 0.1 copy.17
  9.1 0.1 mul.36
  9.2 0.2 fusion.21
  9.5 6.4 %scatter_custom_fusion = bf16[1024,512]{1,0:T(8,128)(2,1)S(1)} fusion(s32[512]{0:T(512)S(1)} %bitcast.49, bf16[256,512]{1,0:T(8,128)(2,1)} %param.6, s32[1024]{0:T(1024)S(1)} %pad_clamp_fusion.1, bf16[]{:T(256)} %constant.26.clone.1), kind=kCustom, calls=%fused_computation.16 | custom fusion | bytes 1049088 | tf_op jit(solution)/shard_map/scatter | solution.py:25
  15.9 75.5 %all_to_all.21 = bf16[128,1,8,512]{3,2,1,0:T(8,128)(2,1)} all-to-all(bf16[128,1,8,512]{3,2,1,0:T(8,128)(2,1)S(1)} %bitcast.44), channel_id=1, replica_groups=mesh['dp'=128,'tensor'=4] {'dp'}, dimensions={0} | all-to-all | bytes 2097152 | tf_op jit(solution)/shard_map/all_to_all | solution.py:29
  91.4 0.0 all-gather.3.cloned.1.call-update
  91.4 0.2 reduce-scatter.2.cloned.1.call-start
  91.7 47.5 %all-gather.3.cloned.1.call-done = bf16[128,1,8,2048]{3,2,1,0:T(8,128)(2,1)} async-done(((bf16[128,1,8,512]{3,2,1,0:T(8,128)(2,1)}), bf16[128,1,8,2048]{3,2,1,0:T(8,128)(2,1)}) %all-gather.3.cloned.1.call-update) | async-done | bytes 4194320 | tf_op jit(solution)/shard_map/all_gather | solution.py:28
  139.2 0.0 copy-done.3
  139.2 3.6 %fusion.2 = f32[1024,256]{1,0:T(8,128)S(1)} fusion(bf16[128,1,8,2048]{3,2,1,0:T(8,128)(2,1)} %all-gather.3.cloned.1.call-done, bf16[1,2048,256]{2,1,0:T(8,128)(2,1)S(1)} %copy-done.3), kind=kOutput, calls=%fused_computation.5 | convolution fusion | flops 1073741824 | bytes 6291456 | tf_op jit(solution)/shard_map/dot_general | solution.py:36
  142.8 0.0 copy-done.4
  142.8 0.0 copy-done.2
  142.8 1.3 fusion.10
  144.1 0.0 copy-done
  144.1 3.2 %convert_bitcast_fusion = bf16[1,128,8,2048]{3,1,2,0:T(8,128)(2,1)} fusion(bf16[1,256,2048]{2,1,0:T(8,128)(2,1)S(1)} %copy-done, bf16[128,8,256]{2,1,0:T(8,128)(2,1)S(1)} %fusion.10), kind=kOutput, calls=%fused_computation.7 | convolution fusion | flops 1075838976 | bytes 5767168 | tf_op jit(solution)/shard_map/dot_general | solution.py:39
  147.3 0.0 reduce-scatter.2.cloned.1.call-update
  147.4 55.1 %reduce-scatter.2.cloned.1.call-done = bf16[1,128,8,512]{3,1,2,0:T(8,128)(2,1)} async-done(((bf16[1,128,8,2048]{3,1,2,0:T(8,128)(2,1)}), bf16[1,128,8,512]{3,1,2,0:T(8,128)(2,1)}) %reduce-scatter.2.cloned.1.call-update) | async-done | bytes 1048592 | tf_op jit(solution)/shard_map/reduce_scatter | solution.py:42
  202.4 2.8 copy.23
  205.2 16.6 %all-to-all-start.1 = ((bf16[1,128,8,512]{3,2,0,1:T(8,128)(2,1)}), bf16[1,128,8,512]{3,2,0,1:T(8,128)(2,1)S(1)}, u32[]{:S(2)}, u32[]{:S(2)}) async-start(bf16[1,128,8,512]{3,2,0,1:T(8,128)(2,1)} %copy.23), calls=%async_computation.2 | async-start | bytes 2097152 | tf_op jit(solution)/shard_map/all_to_all | solution.py:45
  221.8 0.1 copy.24
  222.0 55.9 %all-to-all-done.1 = bf16[1,128,8,512]{3,2,0,1:T(8,128)(2,1)S(1)} async-done(((bf16[1,128,8,512]{3,2,0,1:T(8,128)(2,1)}), bf16[1,128,8,512]{3,2,0,1:T(8,128)(2,1)S(1)}, u32[]{:S(2)}, u32[]{:S(2)}) %all-to-all-start.1) | async-done | bytes 1048608 | tf_op jit(solution)/shard_map/all_to_all | solution.py:45
  277.9 2.0 gather_fusion
  279.9 0.7 reshape.113
  280.5 2.1 multiply_reduce_fusion
  (15 shorter events, 0.1 us)
Async XLA Ops:
  6.5 137.6 %copy-start = (bf16[1,256,2048]{2,1,0:T(8,128)(2,1)S(1)}, bf16[1,256,2048]{2,1,0:T(8,128)(2,1)}, u32[]{:S(2)}) copy-start(bf16[1,256,2048]{2,1,0:T(8,128)(2,1)} %param.11) | copy-start | bytes 3145732
  6.5 132.7 %copy-start.3 = (bf16[1,2048,256]{2,1,0:T(8,128)(2,1)S(1)}, bf16[1,2048,256]{2,1,0:T(8,128)(2,1)}, u32[]{:S(2)}) copy-start(bf16[1,2048,256]{2,1,0:T(8,128)(2,1)} %param.9) | copy-start | bytes 3145732
  6.5 132.7 %all-gather.3.cloned.1.call-start = ((), (), s32[]{:S(2)}) async-start(), calls=%async_computation.4 | async-start | bytes 5242880 | tf_op jit(solution)/shard_map/all_gather | solution.py:28
  91.4 51.4 %copy-start.4 = (bf16[1,2048,256]{2,1,0:T(8,128)(2,1)S(1)}, bf16[1,2048,256]{2,1,0:T(8,128)(2,1)}, u32[]{:S(2)}) copy-start(bf16[1,2048,256]{2,1,0:T(8,128)(2,1)} %param.10) | copy-start | bytes 3145732
  91.4 111.0 %reduce-scatter.2.cloned.1.call-start = ((), (), s32[]{:S(2)}) async-start(), calls=%async_computation.3 | async-start | bytes 5242880 | tf_op jit(solution)/shard_map/reduce_scatter | solution.py:42
  139.2 3.6 %copy-start.2 = (bf16[128,1,8,2048]{3,2,1,0:T(8,128)(2,1)S(1)}, bf16[128,1,8,2048]{3,2,1,0:T(8,128)(2,1)}, u32[]{:S(2)}) copy-start(bf16[128,1,8,2048]{3,2,1,0:T(8,128)(2,1)} %all-gather.3.cloned.1.call-done) | copy-start | bytes 12582916
  147.3 74.5 %copy-start.1 = (f32[256,2]{0,1:T(2,128)S(1)}, f32[256,2]{0,1:T(2,128)}, u32[]{:S(2)}) copy-start(f32[256,2]{0,1:T(2,128)} %param.8) | copy-start | bytes 6148
  205.2 72.7 %all-to-all-start.1 = ((bf16[1,128,8,512]{3,2,0,1:T(8,128)(2,1)}), bf16[1,128,8,512]{3,2,0,1:T(8,128)(2,1)S(1)}, u32[]{:S(2)}, u32[]{:S(2)}) async-start(bf16[1,128,8,512]{3,2,0,1:T(8,128)(2,1)} %copy.23), calls=%async_computation.2 | async-start | bytes 2097152 | tf_op jit(solution)/shard_map/all_to_all | solution.py:45
Sparse Core Ops, SparseCore 0:
  91.6 47.6 all-gather.2
  147.5 54.8 reduce-scatter.1
where the time goes:
time: 290 us; the launch traced here: 289 us
  waiting for transfers between devices  159 us (55%)
  blocking collectives  75.5 us (26%)
  starting transfers between devices  16.8 us (6%)
  local copies, waits for them, and re-layouts  13.6 us (5%)
  between operations  13.6 us (5%)
  matrix products  8.07 us (3%)
  other arithmetic  3.26 us (1%)
    all_to_all x1, blocking collectives, body(): lax.all_to_all(send_buffer, 'dp', split_axis=0, concat_axis=1, tiled=True)  75.5 us
    all_to_all x1, waiting for transfers between devices, body(): lax.all_to_all(reduced, 'dp', split_axis=1, concat_axis=0, tiled=True)  55.9 us
    reduce_scatter x1, waiting for transfers between devices, body(): lax.psum_scatter(partial_out.astype(jnp.bfloat16), 'tensor', scatter_dime...  55.1 us
    all_gather x1, waiting for transfers between devices, body(): lax.all_gather(lax.all_to_all(send_buffer, 'dp', split_axis=0, concat_axi...  47.5 us
    all_to_all x1, starting transfers between devices, body(): lax.all_to_all(reduced, 'dp', split_axis=1, concat_axis=0, tiled=True)  16.6 us
    scatter x1, local copies, waits for them, and re-layouts, body(): send_buffer = jnp.zeros((experts_all * capacity, tokens.shape[1]), jnp.bf...  6.4 us
  transfers between devices with their start and end apart: 3, of which 3 were waited for; matrix products, arithmetic and copies ran while one was open for 0% of the time, Pallas kernels for 0%

commit v1 on v0

--- a/solution.py
+++ b/solution.py
@@ -25,11 +25,17 @@
         .set(source_rows)
     )
     send_buffer = send_buffer.reshape(experts_all, 1, capacity, tokens.shape[1])
-    features = lax.all_gather(
-        lax.all_to_all(send_buffer, "dp", split_axis=0, concat_axis=1, tiled=True),
-        "tensor",
+    features = jnp.concatenate(
+        lax.all_to_all(
+            jnp.stack(
+                [lax.all_to_all(send_buffer, "dp", split_axis=0, concat_axis=1, tiled=True)]
+                * lax.axis_size("tensor")
+            ),
+            "tensor",
+            0,
+            0,
+        ),
         axis=3,
-        tiled=True,
     )
     slot_count = features.shape[2]
     token_rows = features[0].reshape(-1, model_width)

time: 290 us -> 289 us (level)
  waiting for transfers between devices: 159 us -> 102 us
  blocking collectives: 75.5 us -> 127 us
  local copies, waits for them, and re-layouts: 13.6 us -> 20.7 us
    all_to_all x0 -> x1, blocking collectives: none -> 51.3 us  [body(): lax.all_to_all(jnp.stack([lax.all_to_all(send_buffer, 'dp', split_axis=0,...]
    all_gather x1 -> x0, waiting for transfers between devices: 47.5 us -> none  [body(): lax.all_gather(lax.all_to_all(send_buffer, 'dp', split_axis=0, concat_axi...]
    reduce_scatter x1, waiting for transfers between devices: 55.1 us -> 46 us  [body(): lax.psum_scatter(partial_out.astype(jnp.bfloat16), 'tensor', scatter_dime...]
    reshape x0 -> x1, local copies, waits for them, and re-layouts: none -> 5.39 us  [body(): jnp.concatenate(lax.all_to_all(jnp.stack([lax.all_to_all(send_buffer, 'dp...]
  transfers between devices with their start and end apart: 3 -> 2, of which waited for: 3 -> 2; matrix products, arithmetic and copies ran while one was open for 0% -> 0% of each run, Pallas kernels for 0% -> 0%
where the time goes in v1:
time: 289 us
  blocking collectives  127 us (44%)
  waiting for transfers between devices  102 us (35%)
  local copies, waits for them, and re-layouts  20.7 us (7%)
  starting transfers between devices  16.6 us (6%)
  between operations  13.6 us (5%)
  matrix products  5.75 us (2%)
  other arithmetic  3.26 us (1%)
    all_to_all x1, blocking collectives, body(): lax.all_to_all(send_buffer, 'dp', split_axis=0, concat_axis=1, tiled=True)  75.4 us
    all_to_all x1, waiting for transfers between devices, body(): lax.all_to_all(reduced, 'dp', split_axis=1, concat_axis=0, tiled=True)  55.9 us
    all_to_all x1, blocking collectives, body(): lax.all_to_all(jnp.stack([lax.all_to_all(send_buffer, 'dp', split_axis=0,...  51.3 us
    reduce_scatter x1, waiting for transfers between devices, body(): lax.psum_scatter(partial_out.astype(jnp.bfloat16), 'tensor', scatter_dime...  46 us
    all_to_all x1, starting transfers between devices, body(): lax.all_to_all(reduced, 'dp', split_axis=1, concat_axis=0, tiled=True)  16.6 us
    scatter x1, local copies, waits for them, and re-layouts, body(): send_buffer = jnp.zeros((experts_all * capacity, tokens.shape[1]), jnp.bf...  6.4 us
  transfers between devices with their start and end apart: 2, of which 2 were waited for; matrix products, arithmetic and copies ran while one was open for 0% of the time, Pallas kernels for 0%

profile of v1, /device:TPU:2, one launch (start us, length us, event | category | flops | bytes accessed | tf_op | source)
XLA Modules:
  0.0 288.5 jit_solution(9912662370453579189)
XLA Ops:
  6.5 0.0 copy-start
  6.5 0.9 copy.18
  7.4 0.1 eq.29
  7.6 0.1 eq.25
  7.7 0.7 broadcast_multiply_fusion
  8.4 0.1 copy.20
  8.5 0.2 fusion.12
  8.9 0.1 copy.17
  9.0 0.1 mul.36
  9.2 0.2 fusion.11
  9.4 6.4 %scatter_custom_fusion = bf16[1024,512]{1,0:T(8,128)(2,1)S(1)} fusion(s32[512]{0:T(512)S(1)} %bitcast.52, bf16[256,512]{1,0:T(8,128)(2,1)} %param.6, s32[1024]{0:T(1024)S(1)} %pad_clamp_fusion.1, bf16[]{:T(256)} %constant.26.clone.1), kind=kCustom, calls=%fused_computation.14 | custom fusion | bytes 1049088 | tf_op jit(solution)/shard_map/scatter | solution.py:25
  15.8 75.4 %all_to_all.23 = bf16[128,1,8,512]{3,2,1,0:T(8,128)(2,1)S(1)} all-to-all(bf16[128,1,8,512]{3,2,1,0:T(8,128)(2,1)S(1)} %bitcast.47), channel_id=1, replica_groups=mesh['dp'=128,'tensor'=4] {'dp'}, dimensions={0} | all-to-all | bytes 2097152 | tf_op jit(solution)/shard_map/all_to_all | solution.py:31
  91.2 0.3 stack.10
  91.6 51.3 %all_to_all.24 = bf16[4,1,128,8,512]{4,3,2,1,0:T(8,128)(2,1)S(1)} all-to-all(bf16[4,1,128,8,512]{4,3,2,1,0:T(8,128)(2,1)S(1)} %stack.10), channel_id=1, replica_groups=mesh['dp'=128,'tensor'=4] {'tensor'}, dimensions={0} | all-to-all | bytes 8388608 | tf_op jit(solution)/shard_map/all_to_all | solution.py:29
  142.8 5.4 %copy.30 = bf16[1,128,8,4,512]{4,3,2,1,0:T(4,128)(2,1)S(1)} copy(bf16[1,128,8,4,512]{4,2,1,0,3:T(8,128)(2,1)S(1)} %bitcast.42) | data formatting | bytes 8388608 | tf_op jit(solution)/shard_map/reshape | solution.py:28
  148.2 0.0 copy-start.2
  148.2 1.4 copy.26
  149.7 0.0 copy-start.3
  149.7 1.3 fusion.4
  150.9 0.0 copy-done.3
  150.9 1.3 fusion.1
  152.3 0.0 copy-done
  152.3 3.2 %convert_bitcast_fusion = bf16[1,128,8,2048]{3,1,2,0:T(8,128)(2,1)} fusion(bf16[1,256,2048]{2,1,0:T(8,128)(2,1)S(1)} %copy-done, bf16[128,8,256]{2,1,0:T(8,128)(2,1)S(1)} %fusion.1), kind=kOutput, calls=%fused_computation.4 | convolution fusion | flops 1075838976 | bytes 5767168 | tf_op jit(solution)/shard_map/dot_general | solution.py:45
  155.5 0.0 reduce-scatter.2.cloned.1.call-update
  155.5 46.0 %reduce-scatter.2.cloned.1.call-done = bf16[1,128,8,512]{3,1,2,0:T(8,128)(2,1)} async-done(((bf16[1,128,8,2048]{3,1,2,0:T(8,128)(2,1)}), bf16[1,128,8,512]{3,1,2,0:T(8,128)(2,1)}) %reduce-scatter.2.cloned.1.call-update) | async-done | bytes 1048592 | tf_op jit(solution)/shard_map/reduce_scatter | solution.py:48
  201.5 2.8 copy.24
  204.3 16.6 %all-to-all-start.2 = ((bf16[1,128,8,512]{3,2,0,1:T(8,128)(2,1)}), bf16[1,128,8,512]{3,2,0,1:T(8,128)(2,1)S(1)}, u32[]{:S(2)}, u32[]{:S(2)}) async-start(bf16[1,128,8,512]{3,2,0,1:T(8,128)(2,1)} %copy.24), calls=%async_computation.3 | async-start | bytes 2097152 | tf_op jit(solution)/shard_map/all_to_all | solution.py:51
  220.9 0.1 copy.25
  221.0 55.9 %all-to-all-done.2 = bf16[1,128,8,512]{3,2,0,1:T(8,128)(2,1)S(1)} async-done(((bf16[1,128,8,512]{3,2,0,1:T(8,128)(2,1)}), bf16[1,128,8,512]{3,2,0,1:T(8,128)(2,1)S(1)}, u32[]{:S(2)}, u32[]{:S(2)}) %all-to-all-start.2) | async-done | bytes 1048608 | tf_op jit(solution)/shard_map/all_to_all | solution.py:51
  277.0 2.0 gather_fusion
  278.9 0.7 reshape.122
  279.6 2.1 multiply_reduce_fusion
  (14 shorter events, 0.1 us)
Async XLA Ops:
  6.5 145.7 %copy-start = (bf16[1,256,2048]{2,1,0:T(8,128)(2,1)S(1)}, bf16[1,256,2048]{2,1,0:T(8,128)(2,1)}, u32[]{:S(2)}) copy-start(bf16[1,256,2048]{2,1,0:T(8,128)(2,1)} %param.11) | copy-start | bytes 3145732
  6.5 195.0 %reduce-scatter.2.cloned.1.call-start = ((), (), s32[]{:S(2)}) async-start(), calls=%async_computation.4 | async-start | bytes 5242880 | tf_op jit(solution)/shard_map/reduce_scatter | solution.py:48
  148.2 1.4 copy-start.2
  149.7 1.3 copy-start.3
  155.5 65.4 %copy-start.1 = (f32[256,2]{0,1:T(2,128)S(1)}, f32[256,2]{0,1:T(2,128)}, u32[]{:S(2)}) copy-start(f32[256,2]{0,1:T(2,128)} %param.8) | copy-start | bytes 6148
  204.3 72.7 %all-to-all-start.2 = ((bf16[1,128,8,512]{3,2,0,1:T(8,128)(2,1)}), bf16[1,128,8,512]{3,2,0,1:T(8,128)(2,1)S(1)}, u32[]{:S(2)}, u32[]{:S(2)}) async-start(bf16[1,128,8,512]{3,2,0,1:T(8,128)(2,1)} %copy.24), calls=%async_computation.3 | async-start | bytes 2097152 | tf_op jit(solution)/shard_map/all_to_all | solution.py:51
Sparse Core Ops, SparseCore 0:
  155.6 45.8 reduce-scatter.1
